TPU v7x, 512 devices: a whole 4x8x8 slice. The times are simulated.
512 devices in a mesh: row: 16 (over z, core), col: 32 (over y, x).
Axes of the slice: x: 4, y: 8, z: 8, core: 2. Of those that a mesh axis runs over, the one named last changes fastest.
Arguments:
- rhs: bfloat16 [57344, 256], P('row', 'col'), may hold values from -6 to 6
- dinv: bfloat16 [224, 256, 256], P('row'), may hold values from -1 to 2.5, as said below
- blocks: bfloat16 [16, 448, 256, 256], P('row', 'col'), may hold values from -0.046875 to 0.046875
- block_row: int32 [16, 448], P('row', 'col'), may hold values from 0 to 14, as said below
- block_col: int32 [16, 448], P('row', 'col'), may hold values from 0 to 223, as said below
Outputs:
- solution: bfloat16 [57344, 256], P('row', 'col')
Inputs may be any that keep to these rules, and one draw needn't show every extreme that they name: `dinv`: lower triangular with positive diagonal. `block_row`: slots at positions below 8 of a device hold level-1 row supernodes, the others level-2 ones; 14 marks an empty slot. Some device fills all its slots. `block_col`: A live slot's column supernode is congruent to the device's col index modulo 32 and has a lower level than its row supernode; no pair of supernodes is held twice. An empty slot holds the device's col index.
All inputs are finite; a program needn't handle non-finite values.
Results may differ from a plain program's by a relative error of at most 0.028.
Values may be sent and summed in bfloat16 or wider, within the bound.
No kernel may reach another device: no remote copies, remote signals or barrier semaphores. Data moves between devices by JAX's collectives and lax.ppermute only.
A program may use at most 64 MiB of HBM per device.

v0:
```python
import jax
import jax.numpy as jnp
from jax import lax
from jax.sharding import PartitionSpec as P

L0 = 8
L1 = 4
L2 = 2
SLOTS1 = 8


def solve_rows(factor, vector):
    return jnp.einsum(
        "kab,kbn->kan", factor, vector.astype(jnp.bfloat16), preferred_element_type=jnp.float32
    ).astype(jnp.bfloat16)


def solve_cols(factor, vector):
    return jnp.einsum(
        "kab,kan->kbn", factor, vector.astype(jnp.bfloat16), preferred_element_type=jnp.float32
    ).astype(jnp.bfloat16)


def pick_rows(table, index, valid):
    final_row = table.shape[0] - 1
    chosen = lax.dynamic_index_in_dim(table, jnp.clip(index, 0, final_row), 0, keepdims=False)
    return jnp.where(valid, chosen, jnp.zeros_like(chosen))


def forward_level(tiles, row_list, source, first, count, target_part, factor_part):
    product = jnp.einsum("sab,sbn->san", tiles, source, preferred_element_type=jnp.float32)
    onehot = (row_list[:, None] == first + jnp.arange(count, dtype=jnp.int32)[None, :]).astype(
        jnp.float32
    )
    partial_sum = jnp.einsum("sk,san->kan", onehot, product)
    summed = lax.psum(partial_sum.astype(jnp.bfloat16), "col").astype(jnp.float32)
    return solve_rows(factor_part, target_part - summed)


def send_panels(full, first_k, owned):
    pieces = [pick_rows(full, first_k + 0, first_k + 0 < owned)]
    return lax.all_gather(jnp.stack(pieces), "row", axis=0, tiled=True)


def carry_terms(tiles, row_list, known):
    padded = jnp.concatenate([known, jnp.zeros((1,) + known.shape[1:], jnp.bfloat16)])
    chosen = jnp.take(padded, row_list, axis=0)
    return jnp.einsum("sab,san->sbn", tiles, chosen, preferred_element_type=jnp.float32)


def scatter_carry(terms, col_list, owned, col_count, row_count, per_dev):
    slot_target = col_list // owned * per_dev + col_list % owned // col_count
    onehot = (
        slot_target[:, None] == jnp.arange(row_count * per_dev, dtype=jnp.int32)[None, :]
    ).astype(jnp.float32)
    return lax.psum_scatter(
        jnp.einsum("sq,sbn->qbn", onehot, terms).astype(jnp.bfloat16),
        "row",
        scatter_dimension=0,
        tiled=True,
    ).astype(jnp.float32)


def on_device(rhs, dinv, blocks, block_row, block_col):
    row_count = lax.axis_size("row")
    col_count = lax.axis_size("col")
    row_id = lax.axis_index("row")
    col_id = lax.axis_index("col")
    middle = L0 + L1
    owned = L0 + L1 + L2
    per_dev = -(-owned // col_count)
    whole = lax.all_gather(rhs, "col", axis=1, tiled=True)
    height = dinv.shape[1]
    breadth = whole.shape[1]
    part_width = breadth // col_count
    target = whole.reshape(owned, height, breadth).astype(jnp.float32)
    tiles_one = blocks[0, :SLOTS1]
    tiles_two = blocks[0, SLOTS1:]
    rows_one = block_row[0, :SLOTS1]
    rows_two = block_row[0, SLOTS1:]
    cols_one = block_col[0, :SLOTS1]
    cols_two = block_col[0, SLOTS1:]
    cols_all = block_col[0]
    first_k = (col_id - owned * row_id) % col_count
    source_one = cols_one // owned * per_dev + cols_one % owned // col_count
    source_two = cols_two // owned * per_dev + cols_two % owned // col_count
    zeros_low = jnp.zeros((L0, height, breadth), jnp.bfloat16)
    zeros_mid = jnp.zeros((L1, height, breadth), jnp.bfloat16)
    zeros_top = jnp.zeros((L2, height, breadth), jnp.bfloat16)
    y_low = solve_rows(dinv[:L0], target[:L0])
    panels_low = send_panels(jnp.concatenate([y_low, zeros_mid, zeros_top]), first_k, owned)
    y_mid = forward_level(
        tiles_one,
        rows_one,
        jnp.take(panels_low, source_one, axis=0),
        L0,
        L1,
        target[L0:middle],
        dinv[L0:middle],
    )
    panels_mid = send_panels(jnp.concatenate([zeros_low, y_mid, zeros_top]), first_k, owned)
    panels_all = panels_low + panels_mid
    y_top = forward_level(
        tiles_two,
        rows_two,
        jnp.take(panels_all, source_two, axis=0),
        middle,
        L2,
        target[middle:],
        dinv[middle:],
    )
    y_all = jnp.concatenate([y_low, y_mid, y_top])
    x_top = solve_cols(dinv[middle:], y_top)
    terms_two = carry_terms(tiles_two, rows_two, jnp.concatenate([zeros_low, zeros_mid, x_top]))
    local_ks = [first_k + 0]
    factors = [
        lax.dynamic_index_in_dim(dinv, jnp.minimum(local_k, owned - 1), 0, keepdims=True)
        for local_k in local_ks
    ]
    y_owned = [
        pick_rows(y_all, local_k, local_k < owned).astype(jnp.float32) for local_k in local_ks
    ]
    carry_first = scatter_carry(terms_two, cols_two, owned, col_count, row_count, per_dev)
    carry_top = [carry_first[0]]
    mid_slots = L0 + jnp.arange(L1, dtype=jnp.int32)
    member = 0
    x_owned = solve_cols(factors[member], (y_owned[member] - carry_top[member])[None])
    spread = jnp.where(
        (mid_slots == local_ks[member])[:, None, None], x_owned, jnp.zeros_like(x_owned)
    )
    x_mid = lax.psum(spread, "col").astype(jnp.float32).astype(jnp.bfloat16)
    terms_one = carry_terms(tiles_one, rows_one, jnp.concatenate([zeros_low, x_mid, x_top]))
    terms_all = jnp.concatenate([terms_one, terms_two])
    carry_second = scatter_carry(terms_all, cols_all, owned, col_count, row_count, per_dev)
    residues = [y_owned[0] - carry_second[0]]
    outgoing = []
    member = 0
    x_owned = solve_cols(factors[member], residues[member][None])[0]
    outgoing.append(jnp.where(local_ks[member] < L0, x_owned, jnp.zeros_like(x_owned)))
    outgoing = jnp.stack(outgoing).reshape(per_dev, height, col_count, part_width)
    outgoing = outgoing.transpose(2, 0, 1, 3).reshape(col_count, per_dev * height * part_width)
    incoming = lax.all_to_all(outgoing, "col", split_axis=0, concat_axis=0, tiled=True)
    low_ks = jnp.arange(L0, dtype=jnp.int32)
    sources = (row_id * owned + low_ks) % col_count * per_dev + low_ks // col_count
    x_low = jnp.take(incoming, sources, axis=0).reshape(L0, height, part_width)
    upper = lax.dynamic_slice_in_dim(
        jnp.concatenate([x_mid, x_top]), col_id * part_width, part_width, 2
    )
    return jnp.concatenate([x_low, upper]).reshape(owned * height, part_width)


def solution(mesh):
    placed = (
        P("row", "col"),
        P("row", None, None),
        P("row", "col", None, None),
        P("row", "col"),
        P("row", "col"),
    )
    return jax.shard_map(
        on_device, mesh=mesh, in_specs=placed, out_specs=P("row", "col"), check_vma=False
    )
```

profile of v0, /device:TPU:8, one launch (start us, length us, event | category | flops | bytes accessed | tf_op | source)
XLA Modules:
  0.0 870.5 jit_solution(18008842323864152416)
XLA Ops:
  6.5 0.7 all-gather.4.cloned.1.call-update
  7.3 0.6 pad_dynamic-slice_fusion.7
  7.9 88.9 %all-gather.4.cloned.1.call-done = bf16[3584,256]{0,1:T(8,128)(2,1)} async-done(((bf16[3584,8]{0,1:T(8,128)(2,1)}), bf16[3584,256]{0,1:T(8,128)(2,1)}) %all-gather.4.cloned.1.call-update) | async-done | bytes 1835024 | tf_op jit(solution)/shard_map/all_gather | solution.py:72
  96.8 2.3 slice.69
  99.1 1.5 copy.103
  100.6 0.4 convolution_convert_fusion
  101.2 1.0 copy-done.1
  102.1 0.8 copy-done.2
  102.9 1.4 maximum_select_fusion
  104.5 41.9 %all-gather.6.cloned.1.call-done = bf16[16,256,256]{2,1,0:T(8,128)(2,1)} async-done(((bf16[1,256,256]{2,1,0:T(8,128)(2,1)}), bf16[16,256,256]{2,1,0:T(8,128)(2,1)}) %all-gather.6.cloned.1.call-update) | async-done | bytes 2097168 | tf_op jit(solution)/shard_map/all_gather | solution.py:42
  146.4 2.2 gather_fusion
  148.6 2.8 convolution_bitcast_fusion.1
  151.4 1.9 copy.106
  153.3 0.5 fusion.58
  153.7 0.9 copy.145
  154.7 2.1 slice.70
  156.8 1.6 copy.150
  158.4 151.8 %all-reduce.4.cloned.1.call-done = bf16[4,256,256]{2,1,0:T(8,128)(2,1)} async-done(((bf16[4,256,256]{2,1,0:T(8,128)(2,1)}), bf16[4,256,256]{2,1,0:T(8,128)(2,1)}) %all-reduce.4.cloned.1.call-update) | async-done | bytes 524304 | tf_op jit(solution)/shard_map/psum | solution.py:36
  310.2 1.4 fusion
  311.7 1.4 maximum_select_fusion.1
  313.5 41.2 %all-gather.8.cloned.1.call-done = bf16[16,256,256]{2,1,0:T(8,128)(2,1)} async-done(((bf16[1,256,256]{2,1,0:T(8,128)(2,1)}), bf16[16,256,256]{2,1,0:T(8,128)(2,1)}) %all-gather.8.cloned.1.call-update) | async-done | bytes 2097168 | tf_op jit(solution)/shard_map/all_gather | solution.py:42
  354.7 4.2 add.346
  358.9 3.1 gather_fusion.1
  362.0 2.8 convolution_bitcast_fusion.3
  364.8 2.6 copy.111
  367.4 1.7 fusion.54
  369.1 0.7 copy.146
  369.9 0.6 compare_and_fusion
  370.5 1.8 slice.71
  372.3 2.0 copy.149
  374.3 148.0 %all-reduce.6.cloned.1.call-done = bf16[2,256,256]{2,1,0:T(8,128)(2,1)} async-done(((bf16[2,256,256]{2,1,0:T(8,128)(2,1)}), bf16[2,256,256]{2,1,0:T(8,128)(2,1)}) %all-reduce.6.cloned.1.call-update) | async-done | bytes 262160 | tf_op jit(solution)/shard_map/psum | solution.py:36
  522.3 1.4 convolution_convert_fusion.2
  523.7 0.7 copy-done.7
  524.4 0.3 fusion.1
  524.7 0.7 copy-done.4
  525.4 1.6 pad_maximum_fusion.2
  527.0 3.0 gather_fusion.2
  530.1 2.8 convolution_bitcast_fusion.2
  532.9 2.6 copy.118
  535.4 2.1 fusion.46
  537.5 2.0 copy.144
  539.7 1.7 broadcast_select_fusion.2
  541.3 59.4 %reduce-scatter.3.cloned.1.call-done = bf16[1,256,256]{2,1,0:T(8,128)(2,1)} async-done(((bf16[16,256,256]{2,1,0:T(8,128)(2,1)}), bf16[1,256,256]{2,1,0:T(8,128)(2,1)}) %reduce-scatter.3.cloned.1.call-update) | async-done | bytes 131088 | tf_op jit(solution)/shard_map/reduce_scatter | solution.py:56
  600.7 1.2 convolution_convert_fusion.5
  601.9 0.9 broadcast_select_fusion
  603.1 156.6 %all-reduce.8.cloned.1.call-done = bf16[4,256,256]{2,1,0:T(8,128)(2,1)} async-done(((bf16[4,256,256]{2,1,0:T(8,128)(2,1)}), bf16[4,256,256]{2,1,0:T(8,128)(2,1)}) %all-reduce.8.cloned.1.call-update) | async-done | bytes 524304 | tf_op jit(solution)/shard_map/psum | solution.py:131
  759.8 2.6 pad_maximum_fusion.1
  762.4 2.2 gather_fusion.3
  764.6 1.9 convolution_bitcast_fusion
  766.5 1.4 pad_maximum_fusion
  767.8 4.5 copy.121
  772.4 2.3 fusion.42
  774.6 2.0 copy.143
  776.7 61.1 %reduce-scatter.5.cloned.1.call-done = bf16[1,256,256]{2,1,0:T(8,128)(2,1)} async-done(((bf16[16,256,256]{2,1,0:T(8,128)(2,1)}), bf16[1,256,256]{2,1,0:T(8,128)(2,1)}) %reduce-scatter.5.cloned.1.call-update) | async-done | bytes 131088 | tf_op jit(solution)/shard_map/reduce_scatter | solution.py:56
  837.9 1.1 fusion.3
  839.0 0.3 copy.123
  839.4 0.5 broadcast.811
  839.9 1.1 reduce
  841.2 0.7 reshape.589
  841.9 9.8 %all-to-all-start = ((bf16[32,2,1024]{2,1,0:T(2,128)(2,1)}), bf16[32,2,1024]{2,1,0:T(2,128)(2,1)S(1)}, u32[]{:S(2)}, u32[]{:S(2)}) async-start(bf16[32,2,1024]{2,1,0:T(2,128)(2,1)} %reshape.589), calls=%async_computation.2 | async-start | bytes 262144 | tf_op jit(solution)/shard_map/all_to_all | solution.py:142
  852.2 9.2 %all-to-all-done = bf16[32,2,1024]{2,1,0:T(2,128)(2,1)S(1)} async-done(((bf16[32,2,1024]{2,1,0:T(2,128)(2,1)}), bf16[32,2,1024]{2,1,0:T(2,128)(2,1)S(1)}, u32[]{:S(2)}, u32[]{:S(2)}) %all-to-all-start) | async-done | bytes 131104 | tf_op jit(solution)/shard_map/all_to_all | solution.py:142
  861.5 0.6 gather_fusion.4
  862.1 0.6 gather.27
  863.0 0.6 pad_maximum_fusion.7
  (66 shorter events, 2.2 us)
Async XLA Ops:
  6.5 90.3 %all-gather.4.cloned.1.call-start = ((), (), s32[]{:S(2)}) async-start(), calls=%async_computation.3 | async-start | bytes 1892352 | tf_op jit(solution)/shard_map/all_gather | solution.py:72
  7.3 139.1 %all-gather.6.cloned.1.call-start = ((), (), s32[]{:S(2)}) async-start(), calls=%async_computation.4 | async-start | bytes 2228224 | tf_op jit(solution)/shard_map/all_gather | solution.py:42
  7.9 92.7 %copy-start = (bf16[14,256,256]{2,1,0:T(8,128)(2,1)S(1)}, bf16[14,256,256]{2,1,0:T(8,128)(2,1)}, u32[]{:S(2)}) copy-start(bf16[14,256,256]{2,1,0:T(8,128)(2,1)} %param.6) | copy-start | bytes 5505028
  101.1 1.1 copy-start.1
  101.1 3.3 copy-start.10
  101.1 3.4 copy-start.11
  102.1 0.8 copy-start.2
  104.3 205.9 %all-reduce.4.cloned.1.call-start = ((), (), s32[]{:S(2)}) async-start(), calls=%async_computation.5 | async-start | bytes 1048576 | tf_op jit(solution)/shard_map/psum | solution.py:36
  154.6 200.0 %all-gather.8.cloned.1.call-start = ((), (), s32[]{:S(2)}) async-start(), calls=%async_computation.6 | async-start | bytes 2228224 | tf_op jit(solution)/shard_map/all_gather | solution.py:42
  313.1 209.2 %all-reduce.6.cloned.1.call-start = ((), (), s32[]{:S(2)}) async-start(), calls=%async_computation.7 | async-start | bytes 524288 | tf_op jit(solution)/shard_map/psum | solution.py:36
  369.8 230.9 %reduce-scatter.3.cloned.1.call-start = ((), (), s32[]{:S(2)}) async-start(), calls=%async_computation.8 | async-start | bytes 2228224 | tf_op jit(solution)/shard_map/reduce_scatter | solution.py:56
  522.3 3.1 copy-start.3
  523.7 0.7 copy-start.7
  524.7 0.7 copy-start.4
  539.6 220.2 %all-reduce.8.cloned.1.call-start = ((), (), s32[]{:S(2)}) async-start(), calls=%async_computation.9 | async-start | bytes 1048576 | tf_op jit(solution)/shard_map/psum | solution.py:131
  541.3 218.4 %copy-start.5 = (bf16[2,256,256]{2,1,0:T(8,128)(2,1)S(1)}, bf16[2,256,256]{2,1,0:T(8,128)(2,1)}, u32[]{:S(2)}) copy-start(bf16[2,256,256]{2,1,0:T(8,128)(2,1)} %copy-done.4) | copy-start | bytes 786436
  602.8 235.0 %reduce-scatter.5.cloned.1.call-start = ((), (), s32[]{:S(2)}) async-start(), calls=%async_computation.10 | async-start | bytes 2228224 | tf_op jit(solution)/shard_map/reduce_scatter | solution.py:56
  764.6 1.9 copy-start.6
  776.7 61.2 %copy-start.9 = (bf16[1,256,256]{2,1,0:T(8,128)(2,1)S(1)}, bf16[1,256,256]{2,1,0:T(8,128)(2,1)}, u32[]{:S(2)}) copy-start(bf16[1,256,256]{2,1,0:T(8,128)(2,1)} %broadcast_select_fusion.2) | copy-start | bytes 393220
  776.7 75.1 %copy-start.8 = (bf16[4,256,256]{2,1,0:T(8,128)(2,1)S(1)}, bf16[4,256,256]{2,1,0:T(8,128)(2,1)}, u32[]{:S(2)}) copy-start(bf16[4,256,256]{2,1,0:T(8,128)(2,1)} %all-reduce.8.cloned.1.call-done) | copy-start | bytes 1572868
  841.9 19.4 %all-to-all-start = ((bf16[32,2,1024]{2,1,0:T(2,128)(2,1)}), bf16[32,2,1024]{2,1,0:T(2,128)(2,1)S(1)}, u32[]{:S(2)}, u32[]{:S(2)}) async-start(bf16[32,2,1024]{2,1,0:T(2,128)(2,1)} %reshape.589), calls=%async_computation.2 | async-start | bytes 262144 | tf_op jit(solution)/shard_map/all_to_all | solution.py:142
Sparse Core Ops, SparseCore 0:
  10.5 86.2 all-gather.3
  104.5 41.8 all-gather.5
  154.8 155.4 all-reduce.3
  313.2 41.4 all-gather.7
  369.9 152.3 all-reduce.5
  539.7 60.9 reduce-scatter.2
  604.5 155.2 all-reduce.7
  776.8 61.0 reduce-scatter.4
where the time goes:
time: 872 us; the launch traced here: 871 us
  waiting for transfers between devices  759 us (87%)
  local copies, waits for them, and re-layouts  46.5 us (5%)
  matrix products  22.5 us (3%)
  other arithmetic  18.2 us (2%)
  between operations  13.9 us (2%)
  starting transfers between devices  10.3 us (1%)
    psum x2, waiting for transfers between devices, forward_level(): lax.psum(partial_sum.astype(jnp.bfloat16), 'col').astype(jnp.float32)  300 us
    psum x1, waiting for transfers between devices, on_device(): x_mid = lax.psum(spread, 'col').astype(jnp.float32).astype(jnp.bfloat16)  157 us
    reduce_scatter x2, waiting for transfers between devices, scatter_carry(): lax.psum_scatter(jnp.einsum('sq,sbn->qbn', onehot, terms).astype(jnp.bflo...  121 us
    all_gather x1, waiting for transfers between devices, on_device(): whole = lax.all_gather(rhs, 'col', axis=1, tiled=True)  88.9 us
    all_gather x2, waiting for transfers between devices, send_panels(): return lax.all_gather(jnp.stack(pieces), 'row', axis=0, tiled=True)  83.1 us
  transfers between devices with their start and end apart: 9, of which 9 were waited for; matrix products, arithmetic and copies ran while one was open for 1% of the time, Pallas kernels for 0%

commit v1 on v0

--- a/solution.py
+++ b/solution.py
@@ -7,6 +7,19 @@
 L1 = 4
 L2 = 2
 SLOTS1 = 8
+
+
+def ring_gather(x, axis, dim):
+    ways = lax.axis_size(axis)
+    up = [(d, (d + 1) % ways) for d in range(ways)]
+    down = [(d, (d - 1) % ways) for d in range(ways)]
+    earlier, later = ([x], [x])
+    for _ in range(ways // 2):
+        earlier.append(lax.ppermute(earlier[-1], axis, up))
+    for _ in range((ways - 1) // 2):
+        later.append(lax.ppermute(later[-1], axis, down))
+    line = jnp.concatenate([*earlier[::-1], *later[1:]], axis=dim)
+    return jnp.roll(line, (lax.axis_index(axis) - ways // 2) * x.shape[dim], axis=dim)
 
 
 def solve_rows(factor, vector):
@@ -39,7 +52,7 @@
 
 def send_panels(full, first_k, owned):
     pieces = [pick_rows(full, first_k + 0, first_k + 0 < owned)]
-    return lax.all_gather(jnp.stack(pieces), "row", axis=0, tiled=True)
+    return ring_gather(jnp.stack(pieces), "row", 0)
 
 
 def carry_terms(tiles, row_list, known):

time: 872 us -> 889 us (1.019)
  starting transfers between devices: 10.3 us -> 52.6 us
  waiting for transfers between devices: 759 us -> 722 us
  local copies, waits for them, and re-layouts: 46.5 us -> 55.5 us
    all_gather x2 -> x0, waiting for transfers between devices: 83.1 us -> none  [send_panels(): return lax.all_gather(jnp.stack(pieces), 'row', axis=0, tiled=True)]
    ppermute x0 -> x30, waiting for transfers between devices: none -> 45.4 us  [the longest x16 41 us: ring_gather(): earlier.append(lax.ppermute(earlier[-1], axis, up))]
    ppermute x0 -> x30, starting transfers between devices: none -> 42.3 us  [the longest x14 42.2 us: ring_gather(): later.append(lax.ppermute(later[-1], axis, down))]
    unnamed x30 -> x94, local copies, waits for them, and re-layouts: 7.88 us -> 17.9 us
  transfers between devices with their start and end apart: 9 -> 37, of which waited for: 9 -> 27; matrix products, arithmetic and copies ran while one was open for 1% -> 2% of each run, Pallas kernels for 0% -> 0%
where the time goes in v1:
time: 889 us; the launch traced here: 888 us
  waiting for transfers between devices  722 us (81%)
  local copies, waits for them, and re-layouts  55.5 us (6%)
  starting transfers between devices  52.6 us (6%)
  matrix products  23.8 us (3%)
  other arithmetic  20 us (2%)
  between operations  14.3 us (2%)
    psum x2, waiting for transfers between devices, forward_level(): lax.psum(partial_sum.astype(jnp.bfloat16), 'col').astype(jnp.float32)  300 us
    psum x1, waiting for transfers between devices, on_device(): x_mid = lax.psum(spread, 'col').astype(jnp.float32).astype(jnp.bfloat16)  157 us
    reduce_scatter x2, waiting for transfers between devices, scatter_carry(): lax.psum_scatter(jnp.einsum('sq,sbn->qbn', onehot, terms).astype(jnp.bflo...  121 us
    all_gather x1, waiting for transfers between devices, on_device(): whole = lax.all_gather(rhs, 'col', axis=1, tiled=True)  88.9 us
    ppermute x14, starting transfers between devices, ring_gather(): later.append(lax.ppermute(later[-1], axis, down))  42.2 us
    ppermute x16, waiting for transfers between devices, ring_gather(): earlier.append(lax.ppermute(earlier[-1], axis, up))  41 us
    unnamed x94, local copies, waits for them, and re-layouts  17.9 us
  transfers between devices with their start and end apart: 37, of which 27 were waited for; matrix products, arithmetic and copies ran while one was open for 2% of the time, Pallas kernels for 0%

profile of v1, /device:TPU:8, one launch (start us, length us, event | category | flops | bytes accessed | tf_op | source)
XLA Modules:
  0.0 888.0 jit_solution(15441171927588712333)
XLA Ops:
  7.9 88.9 %all-gather.2.cloned.1.call-done = bf16[3584,256]{0,1:T(8,128)(2,1)} async-done(((bf16[3584,8]{0,1:T(8,128)(2,1)}), bf16[3584,256]{0,1:T(8,128)(2,1)}) %all-gather.2.cloned.1.call-update) | async-done | bytes 1835024 | tf_op jit(solution)/shard_map/all_gather | solution.py:85
  99.4 1.7 convolution_convert_fusion
  102.0 5.6 collective-permute-done
  107.6 3.0 collective-permute-start.8
  110.6 2.6 collective-permute-done.1
  113.9 2.9 collective-permute-start.9
  116.8 2.0 collective-permute-done.2
  119.3 3.1 collective-permute-start.10
  122.4 2.0 collective-permute-done.3
  125.6 3.0 collective-permute-start.11
  131.2 3.1 collective-permute-start.12
  136.8 3.2 collective-permute-start.13
  141.4 1.5 collective-permute-done.13
  142.8 3.1 collective-permute-start.14
  157.9 2.1 fusion.2
  160.0 2.2 gather_fusion
  162.2 2.8 convolution_bitcast_fusion.1
  165.0 1.9 copy.106
  168.3 2.1 slice.70
  170.5 1.6 copy.150
  172.0 152.4 %all-reduce.4.cloned.1.call-done = bf16[4,256,256]{2,1,0:T(8,128)(2,1)} async-done(((bf16[4,256,256]{2,1,0:T(8,128)(2,1)}), bf16[4,256,256]{2,1,0:T(8,128)(2,1)}) %all-reduce.4.cloned.1.call-update) | async-done | bytes 524304 | tf_op jit(solution)/shard_map/psum | solution.py:49
  326.7 5.6 collective-permute-done.15
  332.3 3.0 collective-permute-start.23
  335.2 2.6 collective-permute-done.16
  337.9 3.0 collective-permute-start.24
  340.8 2.6 collective-permute-done.17
  343.6 3.0 collective-permute-start.25
  346.6 2.5 collective-permute-done.18
  349.2 3.0 collective-permute-start.26
  352.2 2.5 collective-permute-done.19
  354.8 3.0 collective-permute-start.27
  357.8 2.5 collective-permute-done.20
  360.4 3.0 collective-permute-start.28
  363.4 2.5 collective-permute-done.21
  365.9 3.1 collective-permute-start.29
  369.0 2.5 collective-permute-done.22
  373.2 2.9 fusion.1
  376.1 3.1 gather_fusion.1
  379.2 2.8 convolution_bitcast_fusion.3
  382.0 2.6 copy.111
  384.6 1.7 fusion.57
  387.9 1.8 slice.71
  389.7 2.1 copy.149
  391.8 147.9 %all-reduce.6.cloned.1.call-done = bf16[2,256,256]{2,1,0:T(8,128)(2,1)} async-done(((bf16[2,256,256]{2,1,0:T(8,128)(2,1)}), bf16[2,256,256]{2,1,0:T(8,128)(2,1)}) %all-reduce.6.cloned.1.call-update) | async-done | bytes 262160 | tf_op jit(solution)/shard_map/psum | solution.py:49
  539.8 1.4 convolution_convert_fusion.2
  542.9 1.6 pad_maximum_fusion.2
  544.5 3.0 gather_fusion.2
  547.5 2.8 convolution_bitcast_fusion.2
  550.3 2.6 copy.118
  552.9 2.1 fusion.49
  555.0 2.1 copy.144
  557.2 1.7 broadcast_select_fusion.2
  558.8 59.4 %reduce-scatter.3.cloned.1.call-done = bf16[1,256,256]{2,1,0:T(8,128)(2,1)} async-done(((bf16[16,256,256]{2,1,0:T(8,128)(2,1)}), bf16[1,256,256]{2,1,0:T(8,128)(2,1)}) %reduce-scatter.3.cloned.1.call-update) | async-done | bytes 131088 | tf_op jit(solution)/shard_map/reduce_scatter | solution.py:69
  620.4 156.6 %all-reduce.8.cloned.1.call-done = bf16[4,256,256]{2,1,0:T(8,128)(2,1)} async-done(((bf16[4,256,256]{2,1,0:T(8,128)(2,1)}), bf16[4,256,256]{2,1,0:T(8,128)(2,1)}) %all-reduce.8.cloned.1.call-update) | async-done | bytes 524304 | tf_op jit(solution)/shard_map/psum | solution.py:144
  777.1 2.7 pad_maximum_fusion.1
  779.8 2.2 gather_fusion.3
  782.0 1.9 convolution_bitcast_fusion
  783.9 1.4 pad_maximum_fusion
  785.3 4.5 copy.121
  789.8 2.3 fusion.45
  792.1 2.1 copy.143
  794.2 61.1 %reduce-scatter.5.cloned.1.call-done = bf16[1,256,256]{2,1,0:T(8,128)(2,1)} async-done(((bf16[16,256,256]{2,1,0:T(8,128)(2,1)}), bf16[1,256,256]{2,1,0:T(8,128)(2,1)}) %reduce-scatter.5.cloned.1.call-update) | async-done | bytes 131088 | tf_op jit(solution)/shard_map/reduce_scatter | solution.py:69
  859.4 9.8 %all-to-all-start = ((bf16[32,2,1024]{2,1,0:T(2,128)(2,1)}), bf16[32,2,1024]{2,1,0:T(2,128)(2,1)S(1)}, u32[]{:S(2)}, u32[]{:S(2)}) async-start(bf16[32,2,1024]{2,1,0:T(2,128)(2,1)} %reshape.589), calls=%async_computation.2 | async-start | bytes 262144 | tf_op jit(solution)/shard_map/all_to_all | solution.py:155
  869.6 9.2 %all-to-all-done = bf16[32,2,1024]{2,1,0:T(2,128)(2,1)S(1)} async-done(((bf16[32,2,1024]{2,1,0:T(2,128)(2,1)}), bf16[32,2,1024]{2,1,0:T(2,128)(2,1)S(1)}, u32[]{:S(2)}, u32[]{:S(2)}) %all-to-all-start) | async-done | bytes 131104 | tf_op jit(solution)/shard_map/all_to_all | solution.py:155
  (189 shorter events, 43.3 us)
Async XLA Ops:
  6.5 90.3 %all-gather.2.cloned.1.call-start = ((), (), s32[]{:S(2)}) async-start(), calls=%async_computation.3 | async-start | bytes 1892352 | tf_op jit(solution)/shard_map/all_gather | solution.py:85
  7.3 317.2 %all-reduce.4.cloned.1.call-start = ((), (), s32[]{:S(2)}) async-start(), calls=%async_computation.4 | async-start | bytes 1048576 | tf_op jit(solution)/shard_map/psum | solution.py:49
  7.9 91.5 %copy-start = (bf16[14,256,256]{2,1,0:T(8,128)(2,1)S(1)}, bf16[14,256,256]{2,1,0:T(8,128)(2,1)}, u32[]{:S(2)}) copy-start(bf16[14,256,256]{2,1,0:T(8,128)(2,1)} %param.8) | copy-start | bytes 5505028
  101.1 52.7 %copy-start.1 = (bf16[8,256,256]{2,1,0:T(8,128)(2,1)}, bf16[8,256,256]{2,1,0:T(8,128)(2,1)S(1)}, u32[]{:S(2)}) copy-start(bf16[8,256,256]{2,1,0:T(8,128)(2,1)S(1)} %convolution_convert_fusion) | copy-start | bytes 3145732
  101.1 23.3 %copy-start.25 = (s32[1,14]{1,0:T(1,128)S(1)}, s32[1,14]{1,0:T(1,128)}, u32[]{:S(2)}) copy-start(s32[1,14]{1,0:T(1,128)} %param.11) | copy-start | bytes 172
  101.1 34.5 %copy-start.27 = (s32[1,14]{1,0:T(1,128)S(1)}, s32[1,14]{1,0:T(1,128)}, u32[]{:S(2)}) copy-start(s32[1,14]{1,0:T(1,128)} %param.10) | copy-start | bytes 172
  101.2 53.3 %copy-start.4 = (bf16[4,256,256]{2,1,0:T(8,128)(2,1)}, bf16[4,256,256]{2,1,0:T(8,128)(2,1)S(1)}, u32[]{:S(2)}) copy-start(bf16[4,256,256]{2,1,0:T(8,128)(2,1)S(1)} %broadcast_in_dim.88) | copy-start | bytes 1572868
  102.0 5.6 collective-permute-start
  107.6 5.6 collective-permute-start.1
  107.6 5.6 collective-permute-start.8
  113.2 6.1 copy-start.14
  113.2 5.6 collective-permute-start.2
  113.9 5.4 collective-permute-start.9
  118.8 5.6 copy-start.17
  118.8 5.6 collective-permute-start.3
  119.3 3.1 copy-start.15
  119.3 5.6 collective-permute-start.10
  124.4 6.8 copy-start.20
  124.4 5.6 collective-permute-start.4
  125.6 5.6 collective-permute-start.11
  130.0 6.8 copy-start.23
  130.0 5.6 collective-permute-start.5
  131.2 3.1 copy-start.21
  131.2 5.6 collective-permute-start.12
  135.6 4.4 copy-start.24
  135.6 5.7 collective-permute-start.6
  136.8 6.0 collective-permute-start.13
  141.3 5.9 collective-permute-start.7
  141.3 13.2 %copy-start.13 = (bf16[1,256,256]{2,1,0:T(8,128)(2,1)S(1)}, bf16[1,256,256]{2,1,0:T(8,128)(2,1)}, u32[]{:S(2)}) copy-start(bf16[1,256,256]{2,1,0:T(8,128)(2,1)} %copy-done.12) | copy-start | bytes 393220
  141.3 13.2 %copy-start.16 = (bf16[1,256,256]{2,1,0:T(8,128)(2,1)S(1)}, bf16[1,256,256]{2,1,0:T(8,128)(2,1)}, u32[]{:S(2)}) copy-start(bf16[1,256,256]{2,1,0:T(8,128)(2,1)} %copy-done.15) | copy-start | bytes 393220
  142.8 13.7 %collective-permute-start.14 = (bf16[1,256,256]{2,1,0:T(8,128)(2,1)}, bf16[1,256,256]{2,1,0:T(8,128)(2,1)S(1)}, u32[]{:S(2)}, u32[]{:S(2)}) collective-permute-start(bf16[1,256,256]{2,1,0:T(8,128)(2,1)} %collective-permute-done.13), channel_id=1, source_target_pairs={{0,480},{32,0},{64,32},{96,64},{128,96},{160,128},{192,160},{224,1... | collective-permute-start | bytes 393224 | tf_op jit(solution)/shard_map/ppermute | solution.py:20
  148.2 6.4 copy-start.19
  149.1 5.5 copy-start.22
  156.5 1.3 copy-start.2
  160.0 2.2 copy-start.29
  168.3 371.5 %all-reduce.6.cloned.1.call-start = ((), (), s32[]{:S(2)}) async-start(), calls=%async_computation.5 | async-start | bytes 524288 | tf_op jit(solution)/shard_map/psum | solution.py:49
  324.5 19.0 %copy-start.26 = (s32[1,14]{1,0:T(1,128)S(1)}, s32[1,14]{1,0:T(1,128)}, u32[]{:S(2)}) copy-start(s32[1,14]{1,0:T(1,128)} %param.11) | copy-start | bytes 172
  324.5 30.2 %copy-start.28 = (s32[1,14]{1,0:T(1,128)S(1)}, s32[1,14]{1,0:T(1,128)}, u32[]{:S(2)}) copy-start(s32[1,14]{1,0:T(1,128)} %param.10) | copy-start | bytes 172
  326.7 5.6 collective-permute-start.15
  332.3 5.6 collective-permute-start.16
  332.3 5.6 collective-permute-start.23
  337.9 5.6 collective-permute-start.17
  337.9 5.7 collective-permute-start.24
  343.5 5.6 collective-permute-start.18
  343.6 5.6 collective-permute-start.25
  349.1 5.6 collective-permute-start.19
  349.2 5.6 collective-permute-start.26
  354.7 5.6 collective-permute-start.20
  354.8 5.6 collective-permute-start.27
  360.3 5.6 collective-permute-start.21
  360.4 5.5 collective-permute-start.28
  365.9 5.6 collective-permute-start.22
  365.9 6.7 collective-permute-start.29
  371.6 1.6 copy-start.3
  387.1 231.1 %reduce-scatter.3.cloned.1.call-start = ((), (), s32[]{:S(2)}) async-start(), calls=%async_computation.6 | async-start | bytes 2228224 | tf_op jit(solution)/shard_map/reduce_scatter | solution.py:69
  539.8 3.1 copy-start.5
  542.2 0.7 copy-start.6
  557.1 220.0 %all-reduce.8.cloned.1.call-start = ((), (), s32[]{:S(2)}) async-start(), calls=%async_computation.7 | async-start | bytes 1048576 | tf_op jit(solution)/shard_map/psum | solution.py:144
  620.3 235.0 %reduce-scatter.5.cloned.1.call-start = ((), (), s32[]{:S(2)}) async-start(), calls=%async_computation.8 | async-start | bytes 2228224 | tf_op jit(solution)/shard_map/reduce_scatter | solution.py:69
  782.0 1.9 copy-start.8
  794.1 61.2 %copy-start.11 = (bf16[1,256,256]{2,1,0:T(8,128)(2,1)S(1)}, bf16[1,256,256]{2,1,0:T(8,128)(2,1)}, u32[]{:S(2)}) copy-start(bf16[1,256,256]{2,1,0:T(8,128)(2,1)} %broadcast_select_fusion.2) | copy-start | bytes 393220
  794.2 75.1 %copy-start.7 = (bf16[2,256,256]{2,1,0:T(8,128)(2,1)S(1)}, bf16[2,256,256]{2,1,0:T(8,128)(2,1)}, u32[]{:S(2)}) copy-start(bf16[2,256,256]{2,1,0:T(8,128)(2,1)} %copy-done.6) | copy-start | bytes 786436
  794.2 75.1 %copy-start.10 = (bf16[4,256,256]{2,1,0:T(8,128)(2,1)S(1)}, bf16[4,256,256]{2,1,0:T(8,128)(2,1)}, u32[]{:S(2)}) copy-start(bf16[4,256,256]{2,1,0:T(8,128)(2,1)} %all-reduce.8.cloned.1.call-done) | copy-start | bytes 1572868
  859.4 19.4 %all-to-all-start = ((bf16[32,2,1024]{2,1,0:T(2,128)(2,1)}), bf16[32,2,1024]{2,1,0:T(2,128)(2,1)S(1)}, u32[]{:S(2)}, u32[]{:S(2)}) async-start(bf16[32,2,1024]{2,1,0:T(2,128)(2,1)} %reshape.589), calls=%async_computation.2 | async-start | bytes 262144 | tf_op jit(solution)/shard_map/all_to_all | solution.py:155
  (3 other events, 2.1 us)
Sparse Core Ops, SparseCore 0:
  10.5 86.2 all-gather.1
  168.4 156.0 all-reduce.3
  387.2 152.4 all-reduce.5
  557.2 60.9 reduce-scatter.2
  621.8 155.2 all-reduce.7
  794.3 61.0 reduce-scatter.4
